TPU v7x, 256 devices: a whole 4x4x8 slice. The times are simulated.
256 devices in a mesh: span: 16 (over x, y_lo, core), sp: 16 (over z, y_hi).
Axes of the slice: x: 4, y: 4 (y_hi: 2, y_lo: 2; y = y_hi * 2 + y_lo), z: 8, core: 2. Of those that a mesh axis runs over, the one named last changes fastest.
Arguments:
- queries: bfloat16 [16, 2048, 3072], P('span', 'sp'), may hold values from -8 to 8
- keys: bfloat16 [16, 2048, 3072], P('span', 'sp'), may hold values from -8 to 8
- values: bfloat16 [16, 2048, 3072], P('span', 'sp'), may hold values from -6 to 6
- cache_keys: bfloat16 [16, 2048, 3072], P('span', None, 'sp'), may hold values from -8 to 8
- cache_values: bfloat16 [16, 2048, 3072], P('span', None, 'sp'), may hold values from -6 to 6
- gate_table: float32 [64, 3072], replicated, may hold values from 0.5 to 2
- prefix_len: int32 [16], P('span'), may hold values from 1 to 2048, as said below
- levels: int32 [16], P('span'), may hold values from 0 to 63
- finisher: int32 [16], replicated, may hold values from 0 to 15, as said below
Outputs:
- attended: bfloat16 [16, 2048, 3072], P('span', 'sp')
Inputs may be any that keep to these rules, and one draw needn't show every extreme that they name: `prefix_len`: the last group's cache is full. `finisher`: a permutation of the 16 group indices whose first entry is below 15.
All inputs are finite; a program needn't handle non-finite values.
Results may differ from a plain program's by a relative error of at most 0.0032.
Values may be sent and summed in bfloat16 or wider, within the bound.
A program may use at most 128 MiB of HBM per device.

v0:
```python
import functools
import math

import jax
import jax.numpy as jnp
from jax import lax
from jax.experimental import pallas as pl
from jax.experimental.pallas import tpu as pltpu
from jax.sharding import PartitionSpec as P

MESH = pl.DeviceIdType.MESH
N = 16
TB = 128
HL = 3
ROWS = 2048
D = 3072
BF = jnp.bfloat16
F32 = jnp.float32
SCALE = 64 ** -0.5 * math.log2(math.e)
BQ = 1024
BK = 1024
NEG = -1e30


def swap(x):
    return jnp.concatenate([x[..., 64:], x[..., :64]], axis=-1)


def low_lanes(shape):
    return lax.broadcasted_iota(jnp.int32, shape, len(shape) - 1) < 64


def kernel(
    q_hbm, k_hbm, v_hbm, ck_hbm, cv_hbm, gate_hbm, plen_ref, level_ref, fin_ref, o_ref,
    q_in, k_in, v_in, ck_in, cv_in, gate_in, gate_row,
    q_pack, kv_pack, q_got, kv_got, kv8, near, pick, part, span_pack, span_got,
    qx, kx, vx, acc_ref, max_ref, out_pack, out_got,
    in_sem, qs, qr, kvs, kvr, s1, r1, s2, r2, s3, r3, os, orr,
):
    sp = lax.axis_index("sp")
    g = lax.axis_index("span")
    newest = fin_ref[0]

    def sp_peer(d):
        return lax.rem(sp + d, N)

    def span_peer(d):
        return lax.rem(g + d, N)

    barrier = pltpu.get_barrier_semaphore()

    def greet(d, _):
        pl.semaphore_signal(barrier, inc=1, device_id={"sp": sp_peer(d)}, device_id_type=MESH)
        pl.semaphore_signal(barrier, inc=1, device_id={"span": span_peer(d)}, device_id_type=MESH)
        return 0

    lax.fori_loop(1, N, greet, 0)

    loads = [
        pltpu.make_async_copy(src, dst, in_sem.at[i])
        for i, (src, dst) in enumerate(
            [
                (q_hbm.at[0], q_in),
                (k_hbm.at[0], k_in),
                (v_hbm.at[0], v_in),
                (ck_hbm.at[0], ck_in),
                (cv_hbm.at[0], cv_in),
                (gate_hbm, gate_in),
            ]
        )
    ]
    for load in loads:
        load.start()

    def wait_bytes(ref, sem):
        pltpu.make_async_copy(ref, ref, sem).wait()

    def to_sp(src_of, dst, send, recv):
        def body(d, _):
            to = sp_peer(d)
            pltpu.make_async_remote_copy(
                src_ref=src_of(to), dst_ref=dst, send_sem=send, recv_sem=recv,
                device_id={"sp": to}, device_id_type=MESH,
            ).start()
            return 0

        lax.fori_loop(1, N, body, 0)

    def to_span(src_of, dst, send, recv):
        def body(d, _):
            to = span_peer(d)
            pltpu.make_async_remote_copy(
                src_ref=src_of(to), dst_ref=dst, send_sem=send, recv_sem=recv,
                device_id={"span": to}, device_id_type=MESH,
            ).start()
            return 0

        lax.fori_loop(1, N, body, 0)

    loads[0].wait()
    low = low_lanes((64, 128))
    for t in range(D // 128):
        x = q_in[:, t * 128 : (t + 1) * 128].astype(F32)
        first, second = x[:64], x[64:]
        even = jnp.where(low, first, swap(second)).astype(BF)
        odd = jnp.where(low, swap(first), second).astype(BF)
        for j, value in ((2 * t, even), (2 * t + 1, odd)):
            q_pack[j % HL, j // HL] = value
    for h in range(HL):
        q_got[h, sp] = q_pack[h, sp]
    pl.semaphore_wait(barrier, 2 * (N - 1))
    for h in range(HL):
        to_sp(lambda to: q_pack.at[h, to], q_got.at[h, sp], qs.at[h], qr.at[h])

    loads[1].wait()
    loads[2].wait()
    low = low_lanes((TB, 128))
    for t in range(D // 128):
        k = k_in[:, t * 128 : (t + 1) * 128].astype(F32)
        v = v_in[:, t * 128 : (t + 1) * 128].astype(F32)
        even = jnp.where(low, k, swap(v)).astype(BF)
        odd = jnp.where(low, swap(k), v).astype(BF)
        for j, value in ((2 * t, even), (2 * t + 1, odd)):
            kv_pack[j % HL, j // HL] = value
    for h in range(HL):
        kv_got[h, sp] = kv_pack[h, sp]

    def send_kv(h):
        to_sp(lambda to: kv_pack.at[h, to], kv_got.at[h, sp], kvs.at[h], kvr.at[h])

    send_kv(0)

    def eight(i, _):
        rows = pl.ds(pl.multiple_of(i * 16, 16), 16)
        k = k_in[rows, :].astype(F32)
        v = v_in[rows, :].astype(F32)
        kv8[2 * i] = jnp.concatenate([k[:8], v[:8]], axis=0).astype(BF)
        kv8[2 * i + 1] = jnp.concatenate([k[8:], v[8:]], axis=0).astype(BF)
        return 0

    lax.fori_loop(0, N // 2, eight, 0)
    near[g] = kv8[g]
    to_span(lambda to: kv8.at[to], near.at[g], s1, r1)

    loads[5].wait()
    low1 = low_lanes((1, 128))
    for h in range(HL):
        j = sp * HL + h
        tile = pl.ds(pl.multiple_of(lax.div(j, 2) * 128, 128), 128)
        chosen = lax.broadcasted_iota(jnp.int32, (64, 128), 0) == level_ref[0]
        row = jnp.sum(jnp.where(chosen, gate_in[:, tile], 0.0), axis=0, keepdims=True)
        odd = lax.rem(j, 2)
        gate_row[h] = jnp.where(jnp.zeros((1, 128), jnp.int32) + odd == 1, swap(row), row)

    loads[3].wait()
    loads[4].wait()
    CH = 256
    low = low_lanes((CH, 128))

    def cache_keys_of(x0, x2, mask):
        r0 = swap(x0)
        return [
            jnp.where(mask, x0, r0),
            jnp.where(mask, r0, x0),
            jnp.concatenate([x2, x2], axis=1),
        ]

    first0 = ck_in[0:16, 0:128].astype(F32)[0:1]
    first2 = ck_in[0:16, 128:192].astype(F32)[0:1]
    first_row = cache_keys_of(first0, first2, low1)

    def cache(i, _):
        rows = pl.ds(pl.multiple_of(i * CH, CH), CH)
        valid = lax.broadcasted_iota(jnp.int32, (CH, 128), 0) + i * CH < plen_ref[0]
        keys = cache_keys_of(ck_in[rows, 0:128].astype(F32), ck_in[rows, 128:192].astype(F32), low)
        v0 = cv_in[rows, 0:128].astype(F32)
        v2 = cv_in[rows, 128:192].astype(F32)
        values = [
            jnp.where(low, v0, 1.0),
            jnp.where(low, swap(v0), 1.0),
            jnp.concatenate([v2, jnp.ones_like(v2)], axis=1),
        ]
        for h in range(HL):
            kx[h, 0, rows, :] = jnp.where(valid, keys[h], first_row[h]).astype(BF)
            vx[h, 0, rows, :] = jnp.where(valid, values[h], 0.0).astype(BF)
        return 0

    lax.fori_loop(0, ROWS // CH, cache, 0)

    def clear(h, _):
        acc_ref[h] = jnp.zeros((ROWS, 128), F32)
        max_ref[h] = jnp.full((ROWS, 128), NEG, F32)
        return 0

    lax.fori_loop(0, HL, clear, 0)

    def take_queries(h):
        wait_bytes(q_got.at[h, pl.ds(0, N - 1)], qr.at[h])
        mask = low_lanes((64, 128))

        def body(b, _):
            x = q_got[h, b].astype(F32) * SCALE
            r = swap(x)

            def pair(top, bottom):
                rest = bottom - bottom.astype(BF).astype(F32)
                return jnp.where(mask, top, rest).astype(BF)

            qx[h, b, 0:64] = pair(x, r)
            qx[h, b, 64:128] = pair(r, x)
            return 0

        lax.fori_loop(0, N, body, 0)

    def take_own(h):
        wait_bytes(kv_got.at[h, pl.ds(0, N - 1)], kvr.at[h])
        mask = low_lanes((TB, 128))

        def body(b, _):
            x = kv_got[h, b].astype(F32)
            r = swap(x)
            rows = pl.ds(pl.multiple_of(b * TB, TB), TB)
            kx[h, 1, rows, :] = jnp.where(mask, x, r).astype(BF)
            vx[h, 1, rows, :] = jnp.where(mask, r, 1.0).astype(BF)
            return 0

        lax.fori_loop(0, N, body, 0)

    def take_newest(h):
        wait_bytes(span_got.at[h, pl.ds(0, N - 1)], r3.at[h])
        mask = low_lanes((TB, 128))
        used = jnp.zeros((TB, 128), jnp.int32) + g > newest
        spare = kx[h, 0, 0:16, :].astype(F32)[0:1]

        def body(b, _):
            x = span_got[h, b].astype(F32)
            r = swap(x)
            rows = pl.ds(pl.multiple_of(b * TB, TB), TB)
            kx[h, 2, rows, :] = jnp.where(used, jnp.where(mask, x, r), spare).astype(BF)
            vx[h, 2, rows, :] = jnp.where(used, jnp.where(mask, r, 1.0), 0.0).astype(BF)
            return 0

        lax.fori_loop(0, N, body, 0)

    def window(s):
        return pl.ds(pl.multiple_of(lax.div(s * HL, 2) * 128, 128), 256)

    def pick_newest():
        wait_bytes(near.at[pl.ds(0, N - 1)], r1)

        def choose(j, kept):
            chosen = jnp.zeros((16, D), jnp.int32) + newest == j
            return jnp.where(chosen, near[j].astype(F32), kept)

        pick[...] = lax.fori_loop(0, N, choose, jnp.zeros((16, D), F32)).astype(BF)
        part[sp] = pick[:, window(sp)]
        to_sp(lambda to: pick.at[:, window(to)], part.at[sp], s2, r2)

    def spread_newest():
        wait_bytes(part.at[pl.ds(0, N - 1)], r2)
        x = part[...].astype(F32)
        k = x[:, :8].reshape(TB, 256)
        v = x[:, 8:].reshape(TB, 256)
        odd = jnp.zeros((TB, 64), jnp.int32) + lax.rem(sp, 2) == 1

        def piece(y, h):
            return jnp.where(odd, y[:, 64 * (h + 1) : 64 * (h + 2)], y[:, 64 * h : 64 * (h + 1)])

        for h in range(HL):
            value = jnp.concatenate([piece(k, h), piece(v, h)], axis=1).astype(BF)
            span_pack[h] = value
            span_got[h, g] = value
        for h in range(HL):
            to_span(lambda to: span_pack.at[h], span_got.at[h, g], s3.at[h], r3.at[h])

    def attend(h, seg, last):
        def block(i, _):
            rows = pl.ds(pl.multiple_of(i * BQ, BQ), BQ)
            blocks = pl.ds(pl.multiple_of(i * (BQ // TB), BQ // TB), BQ // TB)
            q = qx[h, blocks].reshape(BQ, 128)
            m = max_ref[h, rows, 0:1]
            acc = acc_ref[h, rows, :]
            for c in range(ROWS // BK):
                k = kx[h, seg, c * BK : (c + 1) * BK, :]
                v = vx[h, seg, c * BK : (c + 1) * BK, :]
                s = lax.dot_general(q, k, (((1,), (1,)), ((), ())), preferred_element_type=F32)
                top = jnp.maximum(m, jnp.max(s, axis=1, keepdims=True))
                w = jnp.exp2(s - top).astype(BF)
                acc = acc * jnp.exp2(m - top) + jnp.dot(w, v, preferred_element_type=F32)
                m = top
            max_ref[h, rows, :] = jnp.broadcast_to(m, (BQ, 128))
            acc_ref[h, rows, :] = acc

            @pl.when(last)
            def _():
                done = acc_ref[h, rows, :]
                gated = (done / swap(done) * gate_row[h]).reshape(BQ // TB, TB, 128)
                mask = low_lanes((BQ // TB, 64, 128))
                out_pack[h, blocks] = jnp.where(mask, gated[:, :64], swap(gated[:, 64:])).astype(BF)

                def send(b, _):
                    to = i * (BQ // TB) + b

                    @pl.when(to != sp)
                    def _():
                        pltpu.make_async_remote_copy(
                            src_ref=out_pack.at[h, to], dst_ref=out_got.at[h, sp],
                            send_sem=os.at[h], recv_sem=orr.at[h],
                            device_id={"sp": to}, device_id_type=MESH,
                        ).start()

                    @pl.when(to == sp)
                    def _():
                        out_got[h, sp] = out_pack[h, sp]

                    return 0

                lax.fori_loop(0, BQ // TB, send, 0)

            return 0

        lax.fori_loop(0, ROWS // BQ, block, 0)

    order = [(0, 0), (1, 0), (2, 0), (0, 1), (0, 2), (1, 1), (1, 2), (2, 2), (2, 1)]

    def step(i, _):
        @pl.when(i < 3)
        def _():
            take_queries(i)

        @pl.when(i == 2)
        def _():
            pick_newest()
            send_kv(1)
            send_kv(2)

        @pl.when(i == 3)
        def _():
            spread_newest()

        h = jnp.int32(0)
        seg = jnp.int32(0)
        for n, (hn, sn) in enumerate(order):
            h = jnp.where(i == n, hn, h)
            seg = jnp.where(i == n, sn, seg)

        @pl.when(seg == 1)
        def _():
            take_own(h)

        @pl.when(seg == 2)
        def _():
            take_newest(h)

        last = jnp.logical_or(i == 4, jnp.logical_or(i == 6, i == 8))
        attend(h, seg, last)
        return 0

    lax.fori_loop(0, len(order), step, 0)

    for h in range(HL):
        wait_bytes(out_got.at[h, pl.ds(0, N - 1)], orr.at[h])
    low = low_lanes((64, 128))
    for t in range(D // 128):
        j = 2 * t
        a = out_got[j % HL, j // HL].astype(F32)
        b = out_got[(j + 1) % HL, (j + 1) // HL].astype(F32)
        cols = slice(t * 128, (t + 1) * 128)
        o_ref[0, 0:64, cols] = jnp.where(low, a, swap(b)).astype(BF)
        o_ref[0, 64:128, cols] = jnp.where(low, swap(a), b).astype(BF)

    wait_bytes(kv8.at[pl.ds(0, N - 1)], s1)
    wait_bytes(part.at[pl.ds(0, N - 1)], s2)
    for h in range(HL):
        wait_bytes(q_pack.at[h, pl.ds(0, N - 1)], qs.at[h])
        wait_bytes(kv_pack.at[h, pl.ds(0, N - 1)], kvs.at[h])
        wait_bytes(span_got.at[h, pl.ds(0, N - 1)], s3.at[h])
        wait_bytes(out_pack.at[h, pl.ds(0, N - 1)], os.at[h])


def per_device(*args):
    any_ = pl.BlockSpec(memory_space=pl.ANY)
    smem = pl.BlockSpec(memory_space=pltpu.SMEM)
    V = pltpu.VMEM
    dma = pltpu.SemaphoreType.DMA
    return pl.pallas_call(
        kernel,
        out_shape=jax.ShapeDtypeStruct((1, TB, D), BF),
        in_specs=[any_] * 6 + [smem] * 3,
        out_specs=pl.BlockSpec(memory_space=pltpu.VMEM),
        scratch_shapes=[
            V((TB, D), BF), V((TB, D), BF), V((TB, D), BF),
            V((ROWS, HL * 64), BF), V((ROWS, HL * 64), BF), V((64, D), F32), V((HL, 1, 128), F32),
            V((HL, N, 64, 128), BF), V((HL, N, TB, 128), BF),
            V((HL, N, 64, 128), BF), V((HL, N, TB, 128), BF),
            V((N, 16, D), BF), V((N, 16, D), BF), V((16, D), BF), V((N, 16, 256), BF),
            V((HL, TB, 128), BF), V((HL, N, TB, 128), BF),
            V((HL, N, TB, 128), BF), V((HL, 3, ROWS, 128), BF), V((HL, 3, ROWS, 128), BF),
            V((HL, ROWS, 128), F32), V((HL, ROWS, 128), F32),
            V((HL, N, 64, 128), BF), V((HL, N, 64, 128), BF),
            dma((6,)), dma((HL,)), dma((HL,)), dma((HL,)), dma((HL,)),
            dma, dma, dma, dma, dma((HL,)), dma((HL,)), dma((HL,)), dma((HL,)),
        ],
        compiler_params=pltpu.CompilerParams(
            collective_id=0, has_side_effects=True, vmem_limit_bytes=60 * 2**20
        ),
        cost_estimate=pl.CostEstimate(
            flops=9 * 2 * 2 * ROWS * ROWS * 64, bytes_accessed=6 * 2**20,
            transcendentals=9 * ROWS * ROWS,
        ),
    )(*args)


def solution(mesh):
    placed = (
        P("span", "sp", None),
        P("span", "sp", None),
        P("span", "sp", None),
        P("span", None, "sp"),
        P("span", None, "sp"),
        P(),
        P("span"),
        P("span"),
        P(),
    )
    return jax.shard_map(
        per_device, mesh=mesh, in_specs=placed, out_specs=P("span", "sp", None), check_vma=False
    )
```

profile of v0, /device:TPU:202, one launch (start us, length us, event | category | flops | bytes accessed | tf_op | source)
XLA Modules:
  0.0 146.7 jit_solution(612380835715055623)
XLA Ops:
  1.3 0.0 copy-start
  1.3 2.3 %copy.10.ck_hbm = bf16[1,2048,192]{2,1,0:T(8,128)(2,1)} copy(bf16[1,2048,192]{1,2,0:T(8,128)(2,1)} %param.12) | data formatting | bytes 1572864 | tf_op args[3]
  3.6 0.0 copy-done
  3.6 1.3 copy.11.cv_hbm
  4.9 139.7 %shard_map.91 = bf16[1,128,3072]{2,1,0:T(8,128)(2,1)} custom-call(bf16[1,128,3072]{2,1,0:T(8,128)(2,1)} %q_hbm.1, bf16[1,128,3072]{2,1,0:T(8,128)(2,1)} %k_hbm.1, bf16[1,128,3072]{2,1,0:T(8,128)(2,1)} %v_hbm.1, bf16[1,2048,192]{2,1,0:T(8,128)(2,1)} %copy.10.ck_hbm, bf16[1,2048,192]{2,1,0:T(8,128)(2,1)} %copy.11.cv_hbm, f32[64,3072]{1,0:T(8,128)} %gate_hbm.1, ...), custom_call_target="tpu_custom_call" | custom-call | flops 9663676416 | bytes 6291456 | tf_op jit(solution)/shard_map/pallas_call | solution.py:386
  144.6 2.1 %copy.15 = bf16[1,128,3072]{2,1,0:T(8,128)(2,1)} copy(bf16[1,128,3072]{2,1,0:T(8,128)(2,1)} %shard_map.91) | data formatting | bytes 1572864
Async XLA Ops:
  1.3 2.3 %copy-start = (bf16[1,2048,192]{1,2,0:T(8,128)(2,1)S(1)}, bf16[1,2048,192]{1,2,0:T(8,128)(2,1)}, u32[]{:S(2)}) copy-start(bf16[1,2048,192]{1,2,0:T(8,128)(2,1)} %param.13) | copy-start | bytes 2359300
where the time goes:
time: 147 us
  Pallas kernels  140 us (95%)
  local copies, waits for them, and re-layouts  5.68 us (4%)
    pallas_call x1, Pallas kernels, per_device(): pl.pallas_call(kernel, out_shape=jax.ShapeDtypeStruct((1, TB, D), BF), in...  140 us
    unnamed x5, local copies, waits for them, and re-layouts  5.68 us

commit v1 on v0

--- a/solution.py
+++ b/solution.py
@@ -18,12 +18,11 @@
 F32 = jnp.float32
 SCALE = 64 ** -0.5 * math.log2(math.e)
 BQ = 1024
-BK = 1024
 NEG = -1e30
 
 
 def swap(x):
-    return jnp.concatenate([x[..., 64:], x[..., :64]], axis=-1)
+    return pltpu.roll(x, 64, x.ndim - 1)
 
 
 def low_lanes(shape):
@@ -114,14 +113,13 @@
 
     loads[1].wait()
     loads[2].wait()
-    low = low_lanes((TB, 128))
     for t in range(D // 128):
-        k = k_in[:, t * 128 : (t + 1) * 128].astype(F32)
-        v = v_in[:, t * 128 : (t + 1) * 128].astype(F32)
-        even = jnp.where(low, k, swap(v)).astype(BF)
-        odd = jnp.where(low, swap(k), v).astype(BF)
-        for j, value in ((2 * t, even), (2 * t + 1, odd)):
-            kv_pack[j % HL, j // HL] = value
+        k = k_in[:, t * 128 : (t + 1) * 128].T
+        v = v_in[:, t * 128 : (t + 1) * 128].T
+        for j in (2 * t, 2 * t + 1):
+            half = slice(64 * (j - 2 * t), 64 * (j - 2 * t + 1))
+            kv_pack[j % HL, j // HL, 0:64] = k[half]
+            kv_pack[j % HL, j // HL, 64:128] = v[half]
     for h in range(HL):
         kv_got[h, sp] = kv_pack[h, sp]
 
@@ -154,38 +152,31 @@
 
     loads[3].wait()
     loads[4].wait()
-    CH = 256
-    low = low_lanes((CH, 128))
-
-    def cache_keys_of(x0, x2, mask):
-        r0 = swap(x0)
-        return [
-            jnp.where(mask, x0, r0),
-            jnp.where(mask, r0, x0),
-            jnp.concatenate([x2, x2], axis=1),
-        ]
-
-    first0 = ck_in[0:16, 0:128].astype(F32)[0:1]
-    first2 = ck_in[0:16, 128:192].astype(F32)[0:1]
-    first_row = cache_keys_of(first0, first2, low1)
+    def first_key(h):
+        return ck_in[64 * h : 64 * h + 64, 0:128].astype(F32)[:, 0:1]
+
+    spare = [jnp.broadcast_to(first_key(h), (64, 128)) for h in range(HL)]
 
     def cache(i, _):
-        rows = pl.ds(pl.multiple_of(i * CH, CH), CH)
-        valid = lax.broadcasted_iota(jnp.int32, (CH, 128), 0) + i * CH < plen_ref[0]
-        keys = cache_keys_of(ck_in[rows, 0:128].astype(F32), ck_in[rows, 128:192].astype(F32), low)
-        v0 = cv_in[rows, 0:128].astype(F32)
-        v2 = cv_in[rows, 128:192].astype(F32)
-        values = [
-            jnp.where(low, v0, 1.0),
-            jnp.where(low, swap(v0), 1.0),
-            jnp.concatenate([v2, jnp.ones_like(v2)], axis=1),
-        ]
+        lanes = pl.ds(pl.multiple_of(i * 128, 128), 128)
+        valid = lax.broadcasted_iota(jnp.int32, (64, 128), 1) + i * 128 < plen_ref[0]
+        one = jnp.where(valid, 1.0, 0.0).astype(BF)
         for h in range(HL):
-            kx[h, 0, rows, :] = jnp.where(valid, keys[h], first_row[h]).astype(BF)
-            vx[h, 0, rows, :] = jnp.where(valid, values[h], 0.0).astype(BF)
+            k = ck_in[64 * h : 64 * h + 64, lanes].astype(F32)
+            v = cv_in[64 * h : 64 * h + 64, lanes].astype(F32)
+            k = jnp.where(valid, k, spare[h]).astype(BF)
+            kx[h, 0, 0:64, lanes] = k
+            kx[h, 0, 64:128, lanes] = k
+            vx[h, 0, 0:64, lanes] = jnp.where(valid, v, 0.0).astype(BF)
+            vx[h, 0, 64:128, lanes] = one
         return 0
 
-    lax.fori_loop(0, ROWS // CH, cache, 0)
+    lax.fori_loop(0, ROWS // 128, cache, 0)
+    used = jnp.zeros((64, ROWS), jnp.int32) + g > newest
+    one = jnp.where(used, 1.0, 0.0).astype(BF)
+    for h in range(HL):
+        vx[h, 1, 64:128, :] = jnp.ones((64, ROWS), BF)
+        vx[h, 2, 64:128, :] = one
 
     def clear(h, _):
         acc_ref[h] = jnp.zeros((ROWS, 128), F32)
@@ -198,49 +189,37 @@
         wait_bytes(q_got.at[h, pl.ds(0, N - 1)], qr.at[h])
         mask = low_lanes((64, 128))
 
-        def body(b, _):
-            x = q_got[h, b].astype(F32) * SCALE
-            r = swap(x)
-
-            def pair(top, bottom):
-                rest = bottom - bottom.astype(BF).astype(F32)
-                return jnp.where(mask, top, rest).astype(BF)
-
-            qx[h, b, 0:64] = pair(x, r)
-            qx[h, b, 64:128] = pair(r, x)
+        def body(n, _):
+            for b in range(4):
+                b = n * 4 + b
+                x = q_got[h, b].astype(F32) * SCALE
+                r = swap(x)
+                qx[h, b, 0:64] = jnp.where(mask, x, r - r.astype(BF).astype(F32)).astype(BF)
+                qx[h, b, 64:128] = jnp.where(mask, r, x - x.astype(BF).astype(F32)).astype(BF)
             return 0
 
-        lax.fori_loop(0, N, body, 0)
+        lax.fori_loop(0, N // 4, body, 0)
 
     def take_own(h):
         wait_bytes(kv_got.at[h, pl.ds(0, N - 1)], kvr.at[h])
-        mask = low_lanes((TB, 128))
-
-        def body(b, _):
-            x = kv_got[h, b].astype(F32)
-            r = swap(x)
-            rows = pl.ds(pl.multiple_of(b * TB, TB), TB)
-            kx[h, 1, rows, :] = jnp.where(mask, x, r).astype(BF)
-            vx[h, 1, rows, :] = jnp.where(mask, r, 1.0).astype(BF)
-            return 0
-
-        lax.fori_loop(0, N, body, 0)
+        for b in range(N):
+            lanes = slice(b * TB, (b + 1) * TB)
+            k = kv_got[h, b, 0:64]
+            kx[h, 1, 0:64, lanes] = k
+            kx[h, 1, 64:128, lanes] = k
+            vx[h, 1, 0:64, lanes] = kv_got[h, b, 64:128]
 
     def take_newest(h):
         wait_bytes(span_got.at[h, pl.ds(0, N - 1)], r3.at[h])
-        mask = low_lanes((TB, 128))
-        used = jnp.zeros((TB, 128), jnp.int32) + g > newest
-        spare = kx[h, 0, 0:16, :].astype(F32)[0:1]
-
-        def body(b, _):
-            x = span_got[h, b].astype(F32)
-            r = swap(x)
-            rows = pl.ds(pl.multiple_of(b * TB, TB), TB)
-            kx[h, 2, rows, :] = jnp.where(used, jnp.where(mask, x, r), spare).astype(BF)
-            vx[h, 2, rows, :] = jnp.where(used, jnp.where(mask, r, 1.0), 0.0).astype(BF)
-            return 0
-
-        lax.fori_loop(0, N, body, 0)
+        used = jnp.zeros((64, 128), jnp.int32) + g > newest
+        spare = jnp.broadcast_to(kx[h, 0, 0:64, 0:128].astype(F32)[:, 0:1], (64, 128))
+        for b in range(N):
+            lanes = slice(b * TB, (b + 1) * TB)
+            k = jnp.where(used, span_got[h, b, 0:64].astype(F32), spare).astype(BF)
+            v = jnp.where(used, span_got[h, b, 64:128].astype(F32), 0.0).astype(BF)
+            kx[h, 2, 0:64, lanes] = k
+            kx[h, 2, 64:128, lanes] = k
+            vx[h, 2, 0:64, lanes] = v
 
     def window(s):
         return pl.ds(pl.multiple_of(lax.div(s * HL, 2) * 128, 128), 256)
@@ -248,11 +227,16 @@
     def pick_newest():
         wait_bytes(near.at[pl.ds(0, N - 1)], r1)
 
-        def choose(j, kept):
-            chosen = jnp.zeros((16, D), jnp.int32) + newest == j
-            return jnp.where(chosen, near[j].astype(F32), kept)
-
-        pick[...] = lax.fori_loop(0, N, choose, jnp.zeros((16, D), F32)).astype(BF)
+        def choose(n, _):
+            lanes = pl.ds(pl.multiple_of(n * 512, 512), 512)
+            kept = jnp.zeros((16, 512), F32)
+            for j in range(N):
+                chosen = jnp.zeros((16, 512), jnp.int32) + newest == j
+                kept = jnp.where(chosen, near[j, :, lanes].astype(F32), kept)
+            pick[:, lanes] = kept.astype(BF)
+            return 0
+
+        lax.fori_loop(0, D // 512, choose, 0)
         part[sp] = pick[:, window(sp)]
         to_sp(lambda to: pick.at[:, window(to)], part.at[sp], s2, r2)
 
@@ -267,7 +251,7 @@
             return jnp.where(odd, y[:, 64 * (h + 1) : 64 * (h + 2)], y[:, 64 * h : 64 * (h + 1)])
 
         for h in range(HL):
-            value = jnp.concatenate([piece(k, h), piece(v, h)], axis=1).astype(BF)
+            value = jnp.concatenate([piece(k, h), piece(v, h)], axis=1).T.astype(BF)
             span_pack[h] = value
             span_got[h, g] = value
         for h in range(HL):
@@ -278,18 +262,14 @@
             rows = pl.ds(pl.multiple_of(i * BQ, BQ), BQ)
             blocks = pl.ds(pl.multiple_of(i * (BQ // TB), BQ // TB), BQ // TB)
             q = qx[h, blocks].reshape(BQ, 128)
-            m = max_ref[h, rows, 0:1]
+            m = max_ref[h, rows, :]
             acc = acc_ref[h, rows, :]
-            for c in range(ROWS // BK):
-                k = kx[h, seg, c * BK : (c + 1) * BK, :]
-                v = vx[h, seg, c * BK : (c + 1) * BK, :]
-                s = lax.dot_general(q, k, (((1,), (1,)), ((), ())), preferred_element_type=F32)
-                top = jnp.maximum(m, jnp.max(s, axis=1, keepdims=True))
-                w = jnp.exp2(s - top).astype(BF)
-                acc = acc * jnp.exp2(m - top) + jnp.dot(w, v, preferred_element_type=F32)
-                m = top
-            max_ref[h, rows, :] = jnp.broadcast_to(m, (BQ, 128))
-            acc_ref[h, rows, :] = acc
+            s = jnp.dot(q, kx[h, seg], preferred_element_type=F32)
+            top = jnp.maximum(m, jnp.broadcast_to(jnp.max(s, axis=1, keepdims=True), (BQ, 128)))
+            w = jnp.exp2(s - jnp.tile(top, (1, ROWS // 128))).astype(BF)
+            new = lax.dot_general(w, vx[h, seg], (((1,), (1,)), ((), ())), preferred_element_type=F32)
+            max_ref[h, rows, :] = top
+            acc_ref[h, rows, :] = acc * jnp.exp2(m - top) + new
 
             @pl.when(last)
             def _():
@@ -378,7 +358,8 @@
         wait_bytes(out_pack.at[h, pl.ds(0, N - 1)], os.at[h])
 
 
-def per_device(*args):
+def per_device(queries, keys, values, cache_keys, cache_values, *rest):
+    args = (queries, keys, values, cache_keys.swapaxes(1, 2), cache_values.swapaxes(1, 2), *rest)
     any_ = pl.BlockSpec(memory_space=pl.ANY)
     smem = pl.BlockSpec(memory_space=pltpu.SMEM)
     V = pltpu.VMEM
@@ -390,12 +371,12 @@
         out_specs=pl.BlockSpec(memory_space=pltpu.VMEM),
         scratch_shapes=[
             V((TB, D), BF), V((TB, D), BF), V((TB, D), BF),
-            V((ROWS, HL * 64), BF), V((ROWS, HL * 64), BF), V((64, D), F32), V((HL, 1, 128), F32),
+            V((HL * 64, ROWS), BF), V((HL * 64, ROWS), BF), V((64, D), F32), V((HL, 1, 128), F32),
             V((HL, N, 64, 128), BF), V((HL, N, TB, 128), BF),
             V((HL, N, 64, 128), BF), V((HL, N, TB, 128), BF),
             V((N, 16, D), BF), V((N, 16, D), BF), V((16, D), BF), V((N, 16, 256), BF),
             V((HL, TB, 128), BF), V((HL, N, TB, 128), BF),
-            V((HL, N, TB, 128), BF), V((HL, 3, ROWS, 128), BF), V((HL, 3, ROWS, 128), BF),
+            V((HL, N, TB, 128), BF), V((HL, 3, 128, ROWS), BF), V((HL, 3, 128, ROWS), BF),
             V((HL, ROWS, 128), F32), V((HL, ROWS, 128), F32),
             V((HL, N, 64, 128), BF), V((HL, N, 64, 128), BF),
             dma((6,)), dma((HL,)), dma((HL,)), dma((HL,)), dma((HL,)),

time: 147 us -> 114 us (0.78)
  the two profiles are of different devices: /device:TPU:202 before, /device:TPU:198 now
where the time goes in v1:
time: 114 us; the launch traced here: 112 us
  Pallas kernels  108 us (95%)
  local copies, waits for them, and re-layouts  2.06 us (2%)
  between operations  1.3 us (1%)
    pallas_call x1, Pallas kernels, per_device(): pl.pallas_call(kernel, out_shape=jax.ShapeDtypeStruct((1, TB, D), BF), in...  108 us

profile of v1, /device:TPU:198, one launch (start us, length us, event | category | flops | bytes accessed | tf_op | source)
XLA Modules:
  0.0 111.8 jit_solution(15986518566509885271)
XLA Ops:
  1.3 108.4 %shard_map.91 = bf16[1,128,3072]{2,1,0:T(8,128)(2,1)} custom-call(bf16[1,128,3072]{2,1,0:T(8,128)(2,1)} %q_hbm.1, bf16[1,128,3072]{2,1,0:T(8,128)(2,1)} %k_hbm.1, bf16[1,128,3072]{2,1,0:T(8,128)(2,1)} %v_hbm.1, bf16[1,192,2048]{2,1,0:T(8,128)(2,1)} %bitcast.2, bf16[1,192,2048]{2,1,0:T(8,128)(2,1)} %bitcast.3, f32[64,3072]{1,0:T(8,128)} %gate_hbm.1, ...), custom_call_target="tpu_custom_call" | custom-call | flops 9663676416 | bytes 6291456 | tf_op jit(solution)/shard_map/pallas_call | solution.py:367
  109.7 2.1 %copy.13 = bf16[1,128,3072]{2,1,0:T(8,128)(2,1)} copy(bf16[1,128,3072]{2,1,0:T(8,128)(2,1)} %shard_map.91) | data formatting | bytes 1572864

commit v2 on v1

--- a/solution.py
+++ b/solution.py
@@ -19,6 +19,9 @@
 SCALE = 64 ** -0.5 * math.log2(math.e)
 BQ = 1024
 NEG = -1e30
+PICK = 2
+SPREAD = 3
+FORWARD = {4: (0,), 5: (1, 2)}
 
 
 def swap(x):
@@ -32,28 +35,38 @@
 def kernel(
     q_hbm, k_hbm, v_hbm, ck_hbm, cv_hbm, gate_hbm, plen_ref, level_ref, fin_ref, o_ref,
     q_in, k_in, v_in, ck_in, cv_in, gate_in, gate_row,
-    q_pack, kv_pack, q_got, kv_got, kv8, near, pick, part, span_pack, span_got,
+    q_pack, kv_pack, q_got, kv_got, kv8, mate, mine, near, pick, part, span_pack, span_got,
     qx, kx, vx, acc_ref, max_ref, out_pack, out_got,
-    in_sem, qs, qr, kvs, kvr, s1, r1, s2, r2, s3, r3, os, orr,
+    in_sem, qs, qr, kvs, kvr, s0, r0, s1, r1, s2, r2, s3, r3, s4, r4, os, orr,
 ):
     sp = lax.axis_index("sp")
     g = lax.axis_index("span")
     newest = fin_ref[0]
+    core = lax.rem(g, 2)
+    chip = lax.div(g, 2)
+    mate_id = {"span": g + 1 - 2 * core}
 
     def sp_peer(d):
         return lax.rem(sp + d, N)
 
-    def span_peer(d):
-        return lax.rem(g + d, N)
+    def chip_peer(d):
+        return lax.rem(chip + d, N // 2)
 
     barrier = pltpu.get_barrier_semaphore()
 
     def greet(d, _):
         pl.semaphore_signal(barrier, inc=1, device_id={"sp": sp_peer(d)}, device_id_type=MESH)
-        pl.semaphore_signal(barrier, inc=1, device_id={"span": span_peer(d)}, device_id_type=MESH)
         return 0
 
     lax.fori_loop(1, N, greet, 0)
+
+    def greet_chip(d, _):
+        to = {"span": 2 * chip_peer(d) + core}
+        pl.semaphore_signal(barrier, inc=1, device_id=to, device_id_type=MESH)
+        return 0
+
+    lax.fori_loop(1, N // 2, greet_chip, 0)
+    pl.semaphore_signal(barrier, inc=1, device_id=mate_id, device_id_type=MESH)
 
     loads = [
         pltpu.make_async_copy(src, dst, in_sem.at[i])
@@ -85,16 +98,22 @@
 
         lax.fori_loop(1, N, body, 0)
 
-    def to_span(src_of, dst, send, recv):
+    def to_chips(src_of, dst, send, recv):
         def body(d, _):
-            to = span_peer(d)
+            to = chip_peer(d)
             pltpu.make_async_remote_copy(
                 src_ref=src_of(to), dst_ref=dst, send_sem=send, recv_sem=recv,
-                device_id={"span": to}, device_id_type=MESH,
+                device_id={"span": 2 * to + core}, device_id_type=MESH,
             ).start()
             return 0
 
-        lax.fori_loop(1, N, body, 0)
+        lax.fori_loop(1, N // 2, body, 0)
+
+    def to_mate(src, dst, send, recv):
+        pltpu.make_async_remote_copy(
+            src_ref=src, dst_ref=dst, send_sem=send, recv_sem=recv,
+            device_id=mate_id, device_id_type=MESH,
+        ).start()
 
     loads[0].wait()
     low = low_lanes((64, 128))
@@ -107,12 +126,28 @@
             q_pack[j % HL, j // HL] = value
     for h in range(HL):
         q_got[h, sp] = q_pack[h, sp]
-    pl.semaphore_wait(barrier, 2 * (N - 1))
-    for h in range(HL):
+    pl.semaphore_wait(barrier, N - 1 + N // 2)
+
+    def send_q(h):
         to_sp(lambda to: q_pack.at[h, to], q_got.at[h, sp], qs.at[h], qr.at[h])
+
+    send_q(0)
 
     loads[1].wait()
     loads[2].wait()
+
+    def eight(i, _):
+        rows = pl.ds(pl.multiple_of(i * 16, 16), 16)
+        k = k_in[rows, :].astype(F32)
+        v = v_in[rows, :].astype(F32)
+        kv8[0, i] = jnp.concatenate([k[:8], v[:8]], axis=0).astype(BF)
+        kv8[1, i] = jnp.concatenate([k[8:], v[8:]], axis=0).astype(BF)
+        return 0
+
+    lax.fori_loop(0, N // 2, eight, 0)
+    to_mate(kv8.at[1 - core], mate, s0, r0)
+    send_q(1)
+
     for t in range(D // 128):
         k = k_in[:, t * 128 : (t + 1) * 128].T
         v = v_in[:, t * 128 : (t + 1) * 128].T
@@ -126,19 +161,22 @@
     def send_kv(h):
         to_sp(lambda to: kv_pack.at[h, to], kv_got.at[h, sp], kvs.at[h], kvr.at[h])
 
+    send_q(2)
     send_kv(0)
 
-    def eight(i, _):
-        rows = pl.ds(pl.multiple_of(i * 16, 16), 16)
-        k = k_in[rows, :].astype(F32)
-        v = v_in[rows, :].astype(F32)
-        kv8[2 * i] = jnp.concatenate([k[:8], v[:8]], axis=0).astype(BF)
-        kv8[2 * i + 1] = jnp.concatenate([k[8:], v[8:]], axis=0).astype(BF)
-        return 0
-
-    lax.fori_loop(0, N // 2, eight, 0)
-    near[g] = kv8[g]
-    to_span(lambda to: kv8.at[to], near.at[g], s1, r1)
+    wait_bytes(mate, r0)
+
+    def side(i, _):
+        other = jnp.zeros((16, D // 2), jnp.int32) + lax.rem(newest, 2) != core
+        for half in range(2):
+            lanes = slice(half * (D // 2), (half + 1) * (D // 2))
+            own = kv8[core, i, :, lanes].astype(F32)
+            mine[i, :, lanes] = jnp.where(other, mate[i, :, lanes].astype(F32), own).astype(BF)
+        return 0
+
+    lax.fori_loop(0, N // 2, side, 0)
+    near[chip] = mine[chip]
+    to_chips(lambda to: mine.at[to], near.at[chip], s1, r1)
 
     loads[5].wait()
     low1 = low_lanes((1, 128))
@@ -210,13 +248,13 @@
             vx[h, 1, 0:64, lanes] = kv_got[h, b, 64:128]
 
     def take_newest(h):
-        wait_bytes(span_got.at[h, pl.ds(0, N - 1)], r3.at[h])
+        wait_bytes(span_got.at[h, 0], r4.at[h])
         used = jnp.zeros((64, 128), jnp.int32) + g > newest
         spare = jnp.broadcast_to(kx[h, 0, 0:64, 0:128].astype(F32)[:, 0:1], (64, 128))
         for b in range(N):
             lanes = slice(b * TB, (b + 1) * TB)
-            k = jnp.where(used, span_got[h, b, 0:64].astype(F32), spare).astype(BF)
-            v = jnp.where(used, span_got[h, b, 64:128].astype(F32), 0.0).astype(BF)
+            k = jnp.where(used, span_got[h, b % 2, b // 2, 0:64].astype(F32), spare).astype(BF)
+            v = jnp.where(used, span_got[h, b % 2, b // 2, 64:128].astype(F32), 0.0).astype(BF)
             kx[h, 2, 0:64, lanes] = k
             kx[h, 2, 64:128, lanes] = k
             vx[h, 2, 0:64, lanes] = v
@@ -225,13 +263,13 @@
         return pl.ds(pl.multiple_of(lax.div(s * HL, 2) * 128, 128), 256)
 
     def pick_newest():
-        wait_bytes(near.at[pl.ds(0, N - 1)], r1)
+        wait_bytes(near.at[pl.ds(0, N // 2 - 1)], r1)
 
         def choose(n, _):
             lanes = pl.ds(pl.multiple_of(n * 512, 512), 512)
             kept = jnp.zeros((16, 512), F32)
-            for j in range(N):
-                chosen = jnp.zeros((16, 512), jnp.int32) + newest == j
+            for j in range(N // 2):
+                chosen = jnp.zeros((16, 512), jnp.int32) + lax.div(newest, 2) == j
                 kept = jnp.where(chosen, near[j, :, lanes].astype(F32), kept)
             pick[:, lanes] = kept.astype(BF)
             return 0
@@ -253,9 +291,13 @@
         for h in range(HL):
             value = jnp.concatenate([piece(k, h), piece(v, h)], axis=1).T.astype(BF)
             span_pack[h] = value
-            span_got[h, g] = value
+            span_got[h, core, chip] = value
         for h in range(HL):
-            to_span(lambda to: span_pack.at[h], span_got.at[h, g], s3.at[h], r3.at[h])
+            to_chips(lambda to: span_pack.at[h], span_got.at[h, core, chip], s3.at[h], r3.at[h])
+
+    def forward(h):
+        wait_bytes(span_got.at[h, core, pl.ds(0, N // 2 - 1)], r3.at[h])
+        to_mate(span_got.at[h, core], span_got.at[h, core], s4.at[h], r4.at[h])
 
     def attend(h, seg, last):
         def block(i, _):
@@ -301,22 +343,34 @@
 
         lax.fori_loop(0, ROWS // BQ, block, 0)
 
-    order = [(0, 0), (1, 0), (2, 0), (0, 1), (0, 2), (1, 1), (1, 2), (2, 2), (2, 1)]
+    order = [(0, 0), (1, 0), (2, 0), (0, 1), (1, 1), (0, 2), (1, 2), (2, 2), (2, 1)]
 
     def step(i, _):
         @pl.when(i < 3)
         def _():
             take_queries(i)
 
-        @pl.when(i == 2)
+        @pl.when(i == 1)
+        def _():
+            send_kv(1)
+
+        @pl.when(i == PICK)
         def _():
             pick_newest()
-            send_kv(1)
+
+        @pl.when(i == 3)
+        def _():
             send_kv(2)
 
-        @pl.when(i == 3)
+        @pl.when(i == SPREAD)
         def _():
             spread_newest()
+
+        for n, heads in FORWARD.items():
+            @pl.when(i == n)
+            def _():
+                for h in heads:
+                    forward(h)
 
         h = jnp.int32(0)
         seg = jnp.int32(0)
@@ -332,7 +386,7 @@
         def _():
             take_newest(h)
 
-        last = jnp.logical_or(i == 4, jnp.logical_or(i == 6, i == 8))
+        last = jnp.logical_or(i == 5, jnp.logical_or(i == 6, i == 8))
         attend(h, seg, last)
         return 0
 
@@ -349,12 +403,14 @@
         o_ref[0, 0:64, cols] = jnp.where(low, a, swap(b)).astype(BF)
         o_ref[0, 64:128, cols] = jnp.where(low, swap(a), b).astype(BF)
 
-    wait_bytes(kv8.at[pl.ds(0, N - 1)], s1)
+    wait_bytes(mate, s0)
+    wait_bytes(mine.at[pl.ds(0, N // 2 - 1)], s1)
     wait_bytes(part.at[pl.ds(0, N - 1)], s2)
     for h in range(HL):
         wait_bytes(q_pack.at[h, pl.ds(0, N - 1)], qs.at[h])
         wait_bytes(kv_pack.at[h, pl.ds(0, N - 1)], kvs.at[h])
-        wait_bytes(span_got.at[h, pl.ds(0, N - 1)], s3.at[h])
+        wait_bytes(span_got.at[h, 0, pl.ds(0, N // 2 - 1)], s3.at[h])
+        wait_bytes(span_got.at[h, 0], s4.at[h])
         wait_bytes(out_pack.at[h, pl.ds(0, N - 1)], os.at[h])
 
 
@@ -374,13 +430,14 @@
             V((HL * 64, ROWS), BF), V((HL * 64, ROWS), BF), V((64, D), F32), V((HL, 1, 128), F32),
             V((HL, N, 64, 128), BF), V((HL, N, TB, 128), BF),
             V((HL, N, 64, 128), BF), V((HL, N, TB, 128), BF),
-            V((N, 16, D), BF), V((N, 16, D), BF), V((16, D), BF), V((N, 16, 256), BF),
-            V((HL, TB, 128), BF), V((HL, N, TB, 128), BF),
+            V((2, N // 2, 16, D), BF), V((N // 2, 16, D), BF), V((N // 2, 16, D), BF),
+            V((N // 2, 16, D), BF), V((16, D), BF), V((N, 16, 256), BF),
+            V((HL, TB, 128), BF), V((HL, 2, N // 2, TB, 128), BF),
             V((HL, N, TB, 128), BF), V((HL, 3, 128, ROWS), BF), V((HL, 3, 128, ROWS), BF),
             V((HL, ROWS, 128), F32), V((HL, ROWS, 128), F32),
             V((HL, N, 64, 128), BF), V((HL, N, 64, 128), BF),
             dma((6,)), dma((HL,)), dma((HL,)), dma((HL,)), dma((HL,)),
-            dma, dma, dma, dma, dma((HL,)), dma((HL,)), dma((HL,)), dma((HL,)),
+            dma, dma, dma, dma, dma, dma, dma((HL,)), dma((HL,)), dma((HL,)), dma((HL,)), dma((HL,)), dma((HL,)),
         ],
         compiler_params=pltpu.CompilerParams(
             collective_id=0, has_side_effects=True, vmem_limit_bytes=60 * 2**20

time: 114 us -> 106 us (0.930); the launches traced: 112 us -> 105 us
  Pallas kernels: 108 us -> 102 us
    pallas_call x1, Pallas kernels: 108 us -> 102 us  [per_device(): pl.pallas_call(kernel, out_shape=jax.ShapeDtypeStruct((1, TB, D), BF), in...]
where the time goes in v2:
time: 106 us; the launch traced here: 105 us
  Pallas kernels  102 us (96%)
  local copies, waits for them, and re-layouts  2.06 us (2%)
  between operations  1.3 us (1%)
    pallas_call x1, Pallas kernels, per_device(): pl.pallas_call(kernel, out_shape=jax.ShapeDtypeStruct((1, TB, D), BF), in...  102 us

profile of v2, /device:TPU:198, one launch (start us, length us, event | category | flops | bytes accessed | tf_op | source)
XLA Modules:
  0.0 105.4 jit_solution(3857963162228442235)
XLA Ops:
  1.3 102.0 %shard_map.91 = bf16[1,128,3072]{2,1,0:T(8,128)(2,1)} custom-call(bf16[1,128,3072]{2,1,0:T(8,128)(2,1)} %q_hbm.1, bf16[1,128,3072]{2,1,0:T(8,128)(2,1)} %k_hbm.1, bf16[1,128,3072]{2,1,0:T(8,128)(2,1)} %v_hbm.1, bf16[1,192,2048]{2,1,0:T(8,128)(2,1)} %bitcast.2, bf16[1,192,2048]{2,1,0:T(8,128)(2,1)} %bitcast.3, f32[64,3072]{1,0:T(8,128)} %gate_hbm.1, ...), custom_call_target="tpu_custom_call" | custom-call | flops 9663676416 | bytes 6291456 | tf_op jit(solution)/shard_map/pallas_call | solution.py:423
  103.3 2.1 %copy.13 = bf16[1,128,3072]{2,1,0:T(8,128)(2,1)} copy(bf16[1,128,3072]{2,1,0:T(8,128)(2,1)} %shard_map.91) | data formatting | bytes 1572864

commit v3 on v2

--- a/solution.py
+++ b/solution.py
@@ -21,7 +21,7 @@
 NEG = -1e30
 PICK = 2
 SPREAD = 3
-FORWARD = {4: (0,), 5: (1, 2)}
+FORWARD = {4: (0,), 5: (1,), 6: (2,)}
 
 
 def swap(x):
@@ -146,7 +146,6 @@
 
     lax.fori_loop(0, N // 2, eight, 0)
     to_mate(kv8.at[1 - core], mate, s0, r0)
-    send_q(1)
 
     for t in range(D // 128):
         k = k_in[:, t * 128 : (t + 1) * 128].T
@@ -161,8 +160,9 @@
     def send_kv(h):
         to_sp(lambda to: kv_pack.at[h, to], kv_got.at[h, sp], kvs.at[h], kvr.at[h])
 
+    send_kv(0)
+    send_q(1)
     send_q(2)
-    send_kv(0)
 
     wait_bytes(mate, r0)
 
@@ -343,28 +343,18 @@
 
         lax.fori_loop(0, ROWS // BQ, block, 0)
 
-    order = [(0, 0), (1, 0), (2, 0), (0, 1), (1, 1), (0, 2), (1, 2), (2, 2), (2, 1)]
+    order = [(0, 0), (0, 1), (1, 0), (2, 0), (0, 2), (1, 1), (1, 2), (2, 2), (2, 1)]
 
     def step(i, _):
-        @pl.when(i < 3)
-        def _():
-            take_queries(i)
-
-        @pl.when(i == 1)
-        def _():
-            send_kv(1)
-
         @pl.when(i == PICK)
         def _():
             pick_newest()
-
-        @pl.when(i == 3)
-        def _():
-            send_kv(2)
+            send_kv(1)
 
         @pl.when(i == SPREAD)
         def _():
             spread_newest()
+            send_kv(2)
 
         for n, heads in FORWARD.items():
             @pl.when(i == n)
@@ -378,6 +368,10 @@
             h = jnp.where(i == n, hn, h)
             seg = jnp.where(i == n, sn, seg)
 
+        @pl.when(seg == 0)
+        def _():
+            take_queries(h)
+
         @pl.when(seg == 1)
         def _():
             take_own(h)
@@ -386,7 +380,7 @@
         def _():
             take_newest(h)
 
-        last = jnp.logical_or(i == 5, jnp.logical_or(i == 6, i == 8))
+        last = jnp.logical_or(i == 4, jnp.logical_or(i == 6, i == 8))
         attend(h, seg, last)
         return 0
 

time: 106 us -> 99 us (0.934)
  Pallas kernels: 102 us -> 94.2 us
    pallas_call x1, Pallas kernels: 102 us -> 94.2 us  [per_device(): pl.pallas_call(kernel, out_shape=jax.ShapeDtypeStruct((1, TB, D), BF), in...]
where the time goes in v3:
time: 99 us; the launch traced here: 97.6 us
  Pallas kernels  94.2 us (95%)
  local copies, waits for them, and re-layouts  2.06 us (2%)
  between operations  1.3 us (1%)
    pallas_call x1, Pallas kernels, per_device(): pl.pallas_call(kernel, out_shape=jax.ShapeDtypeStruct((1, TB, D), BF), in...  94.2 us
    unnamed x1, local copies, waits for them, and re-layouts  2.06 us

profile of v3, /device:TPU:198, one launch (start us, length us, event | category | flops | bytes accessed | tf_op | source)
XLA Modules:
  0.0 97.6 jit_solution(13691125158098543981)
XLA Ops:
  1.3 94.2 %shard_map.91 = bf16[1,128,3072]{2,1,0:T(8,128)(2,1)} custom-call(bf16[1,128,3072]{2,1,0:T(8,128)(2,1)} %q_hbm.1, bf16[1,128,3072]{2,1,0:T(8,128)(2,1)} %k_hbm.1, bf16[1,128,3072]{2,1,0:T(8,128)(2,1)} %v_hbm.1, bf16[1,192,2048]{2,1,0:T(8,128)(2,1)} %bitcast.2, bf16[1,192,2048]{2,1,0:T(8,128)(2,1)} %bitcast.3, f32[64,3072]{1,0:T(8,128)} %gate_hbm.1, ...), custom_call_target="tpu_custom_call" | custom-call | flops 9663676416 | bytes 6291456 | tf_op jit(solution)/shard_map/pallas_call | solution.py:417
  95.5 2.1 %copy.13 = bf16[1,128,3072]{2,1,0:T(8,128)(2,1)} copy(bf16[1,128,3072]{2,1,0:T(8,128)(2,1)} %shard_map.91) | data formatting | bytes 1572864

commit v4 on v3

--- a/solution.py
+++ b/solution.py
@@ -350,11 +350,11 @@
         def _():
             pick_newest()
             send_kv(1)
+            send_kv(2)
 
         @pl.when(i == SPREAD)
         def _():
             spread_newest()
-            send_kv(2)
 
         for n, heads in FORWARD.items():
             @pl.when(i == n)
@@ -386,16 +386,24 @@
 
     lax.fori_loop(0, len(order), step, 0)
 
-    for h in range(HL):
-        wait_bytes(out_got.at[h, pl.ds(0, N - 1)], orr.at[h])
     low = low_lanes((64, 128))
-    for t in range(D // 128):
+
+    def assemble(t):
         j = 2 * t
         a = out_got[j % HL, j // HL].astype(F32)
         b = out_got[(j + 1) % HL, (j + 1) // HL].astype(F32)
         cols = slice(t * 128, (t + 1) * 128)
         o_ref[0, 0:64, cols] = jnp.where(low, a, swap(b)).astype(BF)
         o_ref[0, 64:128, cols] = jnp.where(low, swap(a), b).astype(BF)
+
+    for h in range(HL):
+        wait_bytes(out_got.at[h, pl.ds(0, N - 1)], orr.at[h])
+        if h == 1:
+            for t in range(0, D // 128, 3):
+                assemble(t)
+    for t in range(D // 128):
+        if t % 3:
+            assemble(t)
 
     wait_bytes(mate, s0)
     wait_bytes(mine.at[pl.ds(0, N // 2 - 1)], s1)

time: 99 us -> 98.6 us (level)
  no operation moved by 1% of the time
where the time goes in v4:
time: 98.6 us; the launch traced here: 97 us
  Pallas kernels  93.6 us (95%)
  local copies, waits for them, and re-layouts  2.06 us (2%)
  between operations  1.3 us (1%)
    pallas_call x1, Pallas kernels, per_device(): pl.pallas_call(kernel, out_shape=jax.ShapeDtypeStruct((1, TB, D), BF), in...  93.6 us
    unnamed x1, local copies, waits for them, and re-layouts  2.06 us

profile of v4, /device:TPU:198, one launch (start us, length us, event | category | flops | bytes accessed | tf_op | source)
XLA Modules:
  0.0 97.0 jit_solution(8344840372125270388)
XLA Ops:
  1.3 93.6 %shard_map.91 = bf16[1,128,3072]{2,1,0:T(8,128)(2,1)} custom-call(bf16[1,128,3072]{2,1,0:T(8,128)(2,1)} %q_hbm.1, bf16[1,128,3072]{2,1,0:T(8,128)(2,1)} %k_hbm.1, bf16[1,128,3072]{2,1,0:T(8,128)(2,1)} %v_hbm.1, bf16[1,192,2048]{2,1,0:T(8,128)(2,1)} %bitcast.2, bf16[1,192,2048]{2,1,0:T(8,128)(2,1)} %bitcast.3, f32[64,3072]{1,0:T(8,128)} %gate_hbm.1, ...), custom_call_target="tpu_custom_call" | custom-call | flops 9663676416 | bytes 6291456 | tf_op jit(solution)/shard_map/pallas_call | solution.py:425
  94.9 2.1 %copy.13 = bf16[1,128,3072]{2,1,0:T(8,128)(2,1)} copy(bf16[1,128,3072]{2,1,0:T(8,128)(2,1)} %shard_map.91) | data formatting | bytes 1572864
